TPU v7x, 32 devices: a whole 2x2x4 slice. The times are simulated.
32 devices in a mesh: lat: 4 (over y, core), lon: 8 (over z, x).
Axes of the slice: x: 2, y: 2, z: 4, core: 2. Of those that a mesh axis runs over, the one named last changes fastest.
Arguments:
- depth: float32 [32, 8192], P('lat', 'lon'), may hold values from 0.5 to 4
- friction: float32 [32, 8192], P('lat', 'lon'), may hold values from 0.2 to 2
- ocean_mask: int32 [32, 8192], P('lat', 'lon'), may hold values 0 or 1
- forcing: float32 [16, 32, 8192], P(None, 'lat', 'lon'), may hold values from -24 to 24
- tile_route: int32 [512, 1], P(('lat', 'lon')), may hold values from 0 to 7; in each aligned block of 16 rows (0 to 15, 16 to 31, ...) at most 2 rows name the same one
- tile_block: int32 [512], P(('lat', 'lon')), may hold values from 0 to 63
- obs_cell: int32 [512, 128], P(('lat', 'lon')), may hold values from 0 to 127
- obs_time: float32 [512, 128], P(('lat', 'lon')), may hold values from 0 to 720
- obs_value: float32 [512, 128], P(('lat', 'lon')), may hold values from -6 to 6
- obs_weight: float32 [512, 128], P(('lat', 'lon')), may hold values from 0.5 to 4
Outputs:
- elevation: float32 [16, 32, 8192], P(None, 'lat', 'lon')
- residual: float32 [16, 32, 8192], P(None, 'lat', 'lon')
Inputs may be any that keep to these rules, and one draw needn't show every extreme that they name: `tile_route`: among the 16 tiles of one device at most 2 name the same owner, and in some device exactly 2 do.
All inputs are finite; a program needn't handle non-finite values. No bound on the sum of `ocean_mask` on one device may be relied on, other than what follows from the above.
Results may differ from a plain program's by a relative error of at most 0.0007.
Values sent between devices are 32-bit elements; how exact they have to be, the bound alone decides.
A program may use at most 64 MiB of HBM per device.

v0:
```python
import math

import jax
import jax.numpy as jnp
from jax import lax
from jax.sharding import PartitionSpec as P

BLOCK = 128
CAP = 2
ITERS = 3
OUTER = 2


OMEGA_DEGREES = (28.984104, 30.0, 28.43973, 30.082137, 15.041069, 13.943036, 14.958931, 13.398661)
HIGHEST = lax.Precision.HIGHEST


def with_halo(array, sides, width, wrap):
    for axis, dim in sides:
        size, length = (lax.axis_size(axis), array.shape[dim])
        up = [(i, (i + 1) % size) for i in range(size if wrap else size - 1)]
        down = [(j, i) for i, j in up]
        last = lax.slice_in_dim(array, length - width, length, axis=dim)
        leading = lax.slice_in_dim(array, 0, width, axis=dim)
        before = lax.ppermute(last, axis, up)
        after = lax.ppermute(leading, axis, down)
        array = jnp.concatenate([before, array, after], axis=dim)
    return array


def angular_rates():
    return jnp.array(OMEGA_DEGREES, dtype=jnp.float32) * (math.pi / 180.0)


def harmonic(first, second):
    return 2.0 * first * second / (first + second)


def neighbours(vector):
    north_south = with_halo(vector, (("lat", 1),), 1, False)
    east_west = with_halo(vector, (("lon", 2),), 1, True)
    east = east_west[:, :, 2:]
    west = east_west[:, :, :-2]
    north = north_south[:, 2:, :]
    south = north_south[:, :-2, :]
    return (east, west, north, south)


def squares(vector):
    return lax.psum(jnp.sum(vector * vector), ("lat", "lon"))


def shards(
    depth,
    friction,
    ocean_mask,
    forcing,
    tile_route,
    tile_block,
    obs_cell,
    obs_time,
    obs_value,
    obs_weight,
):
    channels, rows_dev, cols_dev = forcing.shape
    constituents = channels // 2
    wet = ocean_mask.astype(jnp.float32)
    stacked = jnp.stack([depth, wet])
    extended = with_halo(stacked, (("lat", 1), ("lon", 2)), 1, True)
    lat_place = lax.axis_index("lat")
    lat_count = lax.axis_size("lat")
    low_keep = (lat_place > 0).astype(jnp.float32)
    high_keep = (lat_place < lat_count - 1).astype(jnp.float32)
    depth_ext = extended[0]
    wet_ext = extended[1]
    wet_ext = jnp.concatenate(
        [wet_ext[:1] * low_keep, wet_ext[1:-1], wet_ext[-1:] * high_keep], axis=0
    )
    east_coef = wet * wet_ext[1:-1, 2:] * harmonic(depth, depth_ext[1:-1, 2:])
    west_coef = wet_ext[1:-1, :-2] * wet * harmonic(depth_ext[1:-1, :-2], depth)
    north_coef = wet * wet_ext[2:, 1:-1] * harmonic(depth, depth_ext[2:, 1:-1])
    south_coef = wet_ext[:-2, 1:-1] * wet * harmonic(depth_ext[:-2, 1:-1], depth)
    rates = angular_rates()
    stiff_half = 0.2 * (rates / rates[0]) ** 2
    stiffness = jnp.concatenate([stiff_half, stiff_half])
    owners = lax.axis_size("lon")
    slot_count = owners * CAP
    tile_count, obs_count = obs_cell.shape
    owner_index = tile_route[:, 0]
    owner_hot = (owner_index[:, None] == jnp.arange(owners, dtype=jnp.int32)[None, :]).astype(
        jnp.int32
    )
    earlier = jnp.cumsum(owner_hot, axis=0) - owner_hot
    slot_rank = jnp.sum(earlier * owner_hot, axis=1)
    slot_index = owner_index * CAP + slot_rank
    select = (slot_index[:, None] == jnp.arange(slot_count, dtype=jnp.int32)[None, :]).astype(
        jnp.float32
    )
    positions = (tile_block[:, None] * BLOCK + obs_cell).astype(jnp.float32)
    payload = jnp.stack([obs_time, obs_value, obs_weight, positions], axis=1)
    outgoing = jnp.einsum("ts,tko->sko", select, payload, precision=HIGHEST)
    outgoing = outgoing.reshape(owners, CAP, 4, obs_count)
    incoming = lax.all_to_all(outgoing, "lon", split_axis=0, concat_axis=0, tiled=True).reshape(
        slot_count, 4, obs_count
    )
    obs_times = incoming[:, 0]
    values = incoming[:, 1]
    weights = incoming[:, 2]
    cell_place = incoming[:, 3]
    cell_index = jnp.mod(cell_place, float(BLOCK))
    block_index = (cell_place[:, 0] - cell_index[:, 0]) / float(BLOCK)
    blocks_dev = rows_dev * cols_dev // BLOCK
    block_hot = (block_index[:, None] == jnp.arange(blocks_dev, dtype=jnp.float32)[None, :]).astype(
        jnp.float32
    )
    cell_hot = (
        cell_index[:, :, None] == jnp.arange(BLOCK, dtype=jnp.float32)[None, None, :]
    ).astype(jnp.float32)
    angles = rates[None, :, None] * obs_times[:, None, :]
    basis = jnp.concatenate([jnp.cos(angles), jnp.sin(angles)], axis=1)

    def spread(contrib):
        cell_sums = jnp.einsum("sco,sok->sck", contrib, cell_hot, precision=HIGHEST)
        gridded = jnp.einsum("sb,sck->cbk", block_hot, cell_sums, precision=HIGHEST)
        return gridded.reshape(channels, rows_dev, cols_dev)

    def observe(vector):
        block_field = jnp.einsum(
            "sb,cbk->sck", block_hot, vector.reshape(channels, blocks_dev, BLOCK), precision=HIGHEST
        )
        at_obs = jnp.einsum("sck,sok->sco", block_field, cell_hot, precision=HIGHEST)
        projected = jnp.sum(basis * at_obs, axis=1)
        return spread((weights * projected)[:, None, :] * basis)

    rhs = wet * forcing + spread((weights * values)[:, None, :] * basis)

    def apply_with(vector, diagonal, sides):
        east, west, north, south = sides
        return (
            diagonal * vector
            + east_coef * (vector - east)
            + west_coef * (vector - west)
            + north_coef * (vector - north)
            + south_coef * (vector - south)
            + observe(vector)
        )

    def operate(vector, diagonal):
        return apply_with(vector, diagonal, neighbours(vector))

    elevation = jnp.zeros((channels, rows_dev, cols_dev), jnp.float32)
    residual = rhs
    for outer_turn in range(OUTER):
        sides = neighbours(elevation)
        east, west, north, south = sides
        east_flux = east_coef * (east - elevation)
        north_flux = north_coef * (north - elevation)
        speed_sq = jnp.sum(east_flux * east_flux + north_flux * north_flux, axis=0)
        drag = friction * jnp.sqrt(1.0 + speed_sq / (2 * constituents))
        diagonal = wet * (stiffness[:, None, None] + drag) + (1.0 - wet)
        residual = rhs - apply_with(elevation, diagonal, sides)
        norm_now = squares(residual)

        def plain_step(iteration, state_tuple):
            solution, remainder, direction, norm_prev = state_tuple
            image = operate(direction, diagonal)
            step_size = norm_prev / lax.psum(jnp.sum(direction * image), ("lat", "lon"))
            solution = solution + step_size * direction
            remainder = remainder - step_size * image
            norm_next = squares(remainder)
            direction = remainder + norm_next / norm_prev * direction
            return (solution, remainder, direction, norm_next)

        elevation, residual, direction, norm_now = lax.fori_loop(
            0, ITERS, plain_step, (elevation, residual, residual, norm_now)
        )
    return (elevation, residual)


def solution(mesh):
    in_specs = (
        P("lat", "lon"),
        P("lat", "lon"),
        P("lat", "lon"),
        P(None, "lat", "lon"),
        P(("lat", "lon"), None),
        P(("lat", "lon")),
        P(("lat", "lon"), None),
        P(("lat", "lon"), None),
        P(("lat", "lon"), None),
        P(("lat", "lon"), None),
    )
    out_specs = (P(None, "lat", "lon"), P(None, "lat", "lon"))
    return jax.shard_map(shards, mesh=mesh, in_specs=in_specs, out_specs=out_specs, check_vma=False)
```

profile of v0, /device:TPU:0, one launch (start us, length us, event | category | flops | bytes accessed | tf_op | source)
XLA Modules:
  0.0 743.9 jit_solution(2433318043748930485)
XLA Ops:
  1.3 2.9 collective-permute-start.14
  4.2 3.0 collective-permute-start.12
  7.4 1.7 collective-permute-start.9
  12.1 3.3 all-to-all-start
  16.1 3.2 collective-permute-start.15
  19.4 4.4 collective-permute-start.11
  23.8 1.4 collective-permute-done.11
  26.5 3.7 collective-permute-done.10
  37.9 2.0 multiply_reduce_fusion.5
  39.9 37.4 %psum.42 = f32[]{:T(128)} all-reduce(f32[]{:T(128)} %get-tuple-element.338), channel_id=1, replica_groups=mesh['lat'=4,'lon'=8] {'lat','lon'}, use_global_device_ids=true, to_apply=%region_5.6 | all-reduce | flops 1 | bytes 8 | tf_op jit(solution)/shard_map/psum | solution.py:50
  78.2 308.3 %while.35 = (s32[]{:T(128)}, f32[16,8,1024]{2,1,0:T(8,128)S(1)}, f32[16,8,1024]{2,1,0:T(8,128)S(1)}, f32[16,8,1024]{2,1,0:T(8,128)S(1)}, f32[]{:T(128)}, /*index...) while((s32[]{:T(128)}, f32[16,8,1024]{2,1,0:T(8,128)S(1)}, ...), condition=%wide.region_12.13_spmd.clone, body=%wide.region_6.12_spmd.clone.sunk | while | flops 156340224 | bytes 11468451 | solution.py:174
  82.2 2.3 collective-permute-start.6
  84.5 2.4 collective-permute-start.7
  87.4 1.8 fusion.241
  91.9 2.0 multiply_reduce_fusion.12
  94.0 42.5 %psum.54 = f32[]{:T(128)} all-reduce(f32[]{:T(128)} %get-tuple-element.616), channel_id=1, replica_groups=mesh['lat'=4,'lon'=8] {'lat','lon'}, use_global_device_ids=true, to_apply=%region_9.9 | all-reduce | flops 1 | bytes 8 | tf_op jit(solution)/shard_map/while/body/eval_jaxpr/psum | solution.py:167
  138.0 41.4 %psum.55 = f32[]{:T(128)} all-reduce(f32[]{:T(128)} %get-tuple-element.618), channel_id=1, replica_groups=mesh['lat'=4,'lon'=8] {'lat','lon'}, use_global_device_ids=true, to_apply=%region_11.11 | all-reduce | flops 1 | bytes 8 | tf_op jit(solution)/shard_map/while/body/eval_jaxpr/psum | solution.py:50
  185.0 2.3 collective-permute-start.6
  187.3 2.4 collective-permute-start.7
  190.2 1.8 fusion.241
  194.7 2.0 multiply_reduce_fusion.12
  196.8 41.8 %psum.54 = f32[]{:T(128)} all-reduce(f32[]{:T(128)} %get-tuple-element.616), channel_id=1, replica_groups=mesh['lat'=4,'lon'=8] {'lat','lon'}, use_global_device_ids=true, to_apply=%region_9.9 | all-reduce | flops 1 | bytes 8 | tf_op jit(solution)/shard_map/while/body/eval_jaxpr/psum | solution.py:167
  240.2 42.0 %psum.55 = f32[]{:T(128)} all-reduce(f32[]{:T(128)} %get-tuple-element.618), channel_id=1, replica_groups=mesh['lat'=4,'lon'=8] {'lat','lon'}, use_global_device_ids=true, to_apply=%region_11.11 | all-reduce | flops 1 | bytes 8 | tf_op jit(solution)/shard_map/while/body/eval_jaxpr/psum | solution.py:50
  287.7 2.3 collective-permute-start.6
  290.0 2.4 collective-permute-start.7
  292.9 1.8 fusion.241
  297.5 2.0 multiply_reduce_fusion.12
  299.5 41.8 %psum.54 = f32[]{:T(128)} all-reduce(f32[]{:T(128)} %get-tuple-element.616), channel_id=1, replica_groups=mesh['lat'=4,'lon'=8] {'lat','lon'}, use_global_device_ids=true, to_apply=%region_9.9 | all-reduce | flops 1 | bytes 8 | tf_op jit(solution)/shard_map/while/body/eval_jaxpr/psum | solution.py:167
  342.9 42.0 %psum.55 = f32[]{:T(128)} all-reduce(f32[]{:T(128)} %get-tuple-element.618), channel_id=1, replica_groups=mesh['lat'=4,'lon'=8] {'lat','lon'}, use_global_device_ids=true, to_apply=%region_11.11 | all-reduce | flops 1 | bytes 8 | tf_op jit(solution)/shard_map/while/body/eval_jaxpr/psum | solution.py:50
  386.7 3.3 collective-permute-start.16
  391.4 3.2 collective-permute-start.19
  400.2 40.6 %psum.43 = f32[]{:T(128)} all-reduce(f32[]{:T(128)} %get-tuple-element.336), channel_id=1, replica_groups=mesh['lat'=4,'lon'=8] {'lat','lon'}, use_global_device_ids=true, to_apply=%region_16.17 | all-reduce | flops 1 | bytes 8 | tf_op jit(solution)/shard_map/psum | solution.py:50
  440.9 302.1 %while.34 = (s32[]{:T(128)}, f32[16,8,1024]{2,1,0:T(8,128)S(1)}, f32[16,8,1024]{2,1,0:T(8,128)S(1)}, f32[16,8,1024]{2,1,0:T(8,128)S(1)}, f32[]{:T(128)}, /*index...) while((s32[]{:T(128)}, f32[16,8,1024]{2,1,0:T(8,128)S(1)}, ...), condition=%wide.region_23.24_spmd.clone, body=%wide.region_17.23_spmd.clone.sunk | while | flops 156209152 | bytes 12025529 | solution.py:174
  443.7 2.3 collective-permute-start.2
  446.0 2.4 collective-permute-start.3
  448.9 1.8 fusion.228
  454.6 41.9 %psum.52 = f32[]{:T(128)} all-reduce(f32[]{:T(128)} %get-tuple-element.589), channel_id=1, replica_groups=mesh['lat'=4,'lon'=8] {'lat','lon'}, use_global_device_ids=true, to_apply=%region_20.20 | all-reduce | flops 1 | bytes 8 | tf_op jit(solution)/shard_map/while/body/eval_jaxpr/psum | solution.py:167
  498.1 42.0 %psum.53 = f32[]{:T(128)} all-reduce(f32[]{:T(128)} %get-tuple-element.591), channel_id=1, replica_groups=mesh['lat'=4,'lon'=8] {'lat','lon'}, use_global_device_ids=true, to_apply=%region_22.22 | all-reduce | flops 1 | bytes 8 | tf_op jit(solution)/shard_map/while/body/eval_jaxpr/psum | solution.py:50
  544.4 2.3 collective-permute-start.2
  546.7 2.4 collective-permute-start.3
  549.6 1.8 fusion.228
  555.3 41.5 %psum.52 = f32[]{:T(128)} all-reduce(f32[]{:T(128)} %get-tuple-element.589), channel_id=1, replica_groups=mesh['lat'=4,'lon'=8] {'lat','lon'}, use_global_device_ids=true, to_apply=%region_20.20 | all-reduce | flops 1 | bytes 8 | tf_op jit(solution)/shard_map/while/body/eval_jaxpr/psum | solution.py:167
  598.4 42.3 %psum.53 = f32[]{:T(128)} all-reduce(f32[]{:T(128)} %get-tuple-element.591), channel_id=1, replica_groups=mesh['lat'=4,'lon'=8] {'lat','lon'}, use_global_device_ids=true, to_apply=%region_22.22 | all-reduce | flops 1 | bytes 8 | tf_op jit(solution)/shard_map/while/body/eval_jaxpr/psum | solution.py:50
  645.0 2.3 collective-permute-start.2
  647.3 2.4 collective-permute-start.3
  650.3 1.8 fusion.228
  656.0 41.5 %psum.52 = f32[]{:T(128)} all-reduce(f32[]{:T(128)} %get-tuple-element.589), channel_id=1, replica_groups=mesh['lat'=4,'lon'=8] {'lat','lon'}, use_global_device_ids=true, to_apply=%region_20.20 | all-reduce | flops 1 | bytes 8 | tf_op jit(solution)/shard_map/while/body/eval_jaxpr/psum | solution.py:167
  699.1 42.3 %psum.53 = f32[]{:T(128)} all-reduce(f32[]{:T(128)} %get-tuple-element.591), channel_id=1, replica_groups=mesh['lat'=4,'lon'=8] {'lat','lon'}, use_global_device_ids=true, to_apply=%region_22.22 | all-reduce | flops 1 | bytes 8 | tf_op jit(solution)/shard_map/while/body/eval_jaxpr/psum | solution.py:50
  (254 shorter events, 71.1 us)
Async XLA Ops:
  0.6 6.6 copy-start.11
  1.3 6.0 copy-start.5
  1.3 35.9 %collective-permute-start.14 = (f32[16,8,1]{2,1,0:T(8,128)}, f32[16,8,1]{2,1,0:T(8,128)}, u32[]{:S(2)}, u32[]{:S(2)}) collective-permute-start(f32[16,8,1]{2,1,0:T(8,128)} %broadcast.111), channel_id=1, source_target_pairs={{0,1},{1,2},{2,3},{3,4},{4,5},{5,6},{6,7},{7,0},{8,9},{9,10},{10,1... | collective-permute-start | bytes 1544 | tf_op jit(solution)/shard_map/ppermute | solution.py:25
  4.2 32.1 %collective-permute-start.12 = (f32[16,8,1]{2,1,0:T(8,128)}, f32[16,8,1]{2,1,0:T(8,128)S(1)}, u32[]{:S(2)}, u32[]{:S(2)}) collective-permute-start(f32[16,8,1]{2,1,0:T(8,128)} %broadcast.111), channel_id=1, source_target_pairs={{1,0},{2,1},{3,2},{4,3},{5,4},{6,5},{7,6},{0,7},{9,8},{10,9},{11,1... | collective-permute-start | bytes 1544 | tf_op jit(solution)/shard_map/ppermute | solution.py:26
  7.3 12.0 %collective-permute-start.8 = (f32[2,1,1024]{2,1,0:T(1,128)S(1)}, f32[2,1,1024]{2,1,0:T(1,128)S(1)}, u32[]{:S(2)}, u32[]{:S(2)}) collective-permute-start(f32[2,1,1024]{2,1,0:T(1,128)S(1)} %get-tuple-element.364), channel_id=1, source_target_pairs={{0,8},{8,16},{16,24},{24,0},{1,9},{9,17},{17,25},{25,1},{2,10},{10... | collective-permute-start | bytes 24584 | tf_op jit(solution)/shard_map/ppermute | solution.py:25
  7.4 12.0 %collective-permute-start.9 = (f32[2,1,1024]{2,1,0:T(1,128)S(1)}, f32[2,1,1024]{2,1,0:T(1,128)S(1)}, u32[]{:S(2)}, u32[]{:S(2)}) collective-permute-start(f32[2,1,1024]{2,1,0:T(1,128)S(1)} %get-tuple-element.365), channel_id=1, source_target_pairs={{8,0},{16,8},{24,16},{0,24},{9,1},{17,9},{25,17},{1,25},{10,2},{18... | collective-permute-start | bytes 24584 | tf_op jit(solution)/shard_map/ppermute | solution.py:26
  12.1 18.5 %all-to-all-start = ((f32[8,2,4,128]{3,1,2,0:T(2,128)}), f32[8,2,4,128]{3,1,2,0:T(2,128)S(1)}, u32[]{:S(2)}, u32[]{:S(2)}) async-start(f32[8,2,4,128]{3,1,2,0:T(2,128)} %copy.27), calls=%async_computation | async-start | bytes 65536 | tf_op jit(solution)/shard_map/all_to_all | solution.py:103
  16.1 21.1 %collective-permute-start.15 = (f32[16,1,1024]{2,1,0:T(1,128)}, f32[16,1,1024]{2,1,0:T(1,128)}, u32[]{:S(2)}, u32[]{:S(2)}) collective-permute-start(f32[16,1,1024]{2,1,0:T(1,128)} %broadcast.112), channel_id=1, source_target_pairs={{0,8},{8,16},{16,24},{1,9},{9,17},{17,25},{2,10},{10,18},{18,26},{... | collective-permute-start | bytes 196616 | tf_op jit(solution)/shard_map/ppermute | solution.py:25
  19.4 5.8 collective-permute-start.11
  23.8 6.4 collective-permute-start.10
  25.2 11.1 %collective-permute-start.13 = (f32[16,1,1024]{2,1,0:T(1,128)}, f32[16,1,1024]{2,1,0:T(1,128)S(1)}, u32[]{:S(2)}, u32[]{:S(2)}) collective-permute-start(f32[16,1,1024]{2,1,0:T(1,128)} %broadcast.112), channel_id=1, source_target_pairs={{8,0},{16,8},{24,16},{9,1},{17,9},{25,17},{10,2},{18,10},{26,18},{... | collective-permute-start | bytes 196616 | tf_op jit(solution)/shard_map/ppermute | solution.py:26
  78.9 13.0 %collective-permute-start.4 = (f32[16,1,1024]{2,1,0:T(1,128)}, f32[16,1,1024]{2,1,0:T(1,128)S(1)}, u32[]{:S(2)}, u32[]{:S(2)}) collective-permute-start(f32[16,1,1024]{2,1,0:T(1,128)} %get-tuple-element.611), channel_id=1, source_target_pairs={{0,8},{8,16},{16,24},{1,9},{9,17},{17,25},{2,10},{10,18},{18,26},{... | collective-permute-start | bytes 196616 | tf_op jit(solution)/shard_map/while/body/eval_jaxpr/ppermute | solution.py:25
  80.2 11.7 %collective-permute-start.5 = (f32[16,1,1024]{2,1,0:T(1,128)}, f32[16,1,1024]{2,1,0:T(1,128)S(1)}, u32[]{:S(2)}, u32[]{:S(2)}) collective-permute-start(f32[16,1,1024]{2,1,0:T(1,128)} %get-tuple-element.612), channel_id=1, source_target_pairs={{8,0},{16,8},{24,16},{9,1},{17,9},{25,17},{10,2},{18,10},{26,18},{... | collective-permute-start | bytes 196616 | tf_op jit(solution)/shard_map/while/body/eval_jaxpr/ppermute | solution.py:26
  82.2 9.7 %collective-permute-start.6 = (f32[16,8,1]{2,1,0:T(8,128)}, f32[16,8,1]{2,1,0:T(8,128)S(1)}, u32[]{:S(2)}, u32[]{:S(2)}) collective-permute-start(f32[16,8,1]{2,1,0:T(8,128)} %get-tuple-element.613), channel_id=1, source_target_pairs={{0,1},{1,2},{2,3},{3,4},{4,5},{5,6},{6,7},{7,0},{8,9},{9,10},{10,1... | collective-permute-start | bytes 1544 | tf_op jit(solution)/shard_map/while/body/eval_jaxpr/ppermute | solution.py:25
  84.5 7.4 collective-permute-start.7
  181.7 13.0 %collective-permute-start.4 = (f32[16,1,1024]{2,1,0:T(1,128)}, f32[16,1,1024]{2,1,0:T(1,128)S(1)}, u32[]{:S(2)}, u32[]{:S(2)}) collective-permute-start(f32[16,1,1024]{2,1,0:T(1,128)} %get-tuple-element.611), channel_id=1, source_target_pairs={{0,8},{8,16},{16,24},{1,9},{9,17},{17,25},{2,10},{10,18},{18,26},{... | collective-permute-start | bytes 196616 | tf_op jit(solution)/shard_map/while/body/eval_jaxpr/ppermute | solution.py:25
  183.0 11.7 %collective-permute-start.5 = (f32[16,1,1024]{2,1,0:T(1,128)}, f32[16,1,1024]{2,1,0:T(1,128)S(1)}, u32[]{:S(2)}, u32[]{:S(2)}) collective-permute-start(f32[16,1,1024]{2,1,0:T(1,128)} %get-tuple-element.612), channel_id=1, source_target_pairs={{8,0},{16,8},{24,16},{9,1},{17,9},{25,17},{10,2},{18,10},{26,18},{... | collective-permute-start | bytes 196616 | tf_op jit(solution)/shard_map/while/body/eval_jaxpr/ppermute | solution.py:26
  185.0 9.7 %collective-permute-start.6 = (f32[16,8,1]{2,1,0:T(8,128)}, f32[16,8,1]{2,1,0:T(8,128)S(1)}, u32[]{:S(2)}, u32[]{:S(2)}) collective-permute-start(f32[16,8,1]{2,1,0:T(8,128)} %get-tuple-element.613), channel_id=1, source_target_pairs={{0,1},{1,2},{2,3},{3,4},{4,5},{5,6},{6,7},{7,0},{8,9},{9,10},{10,1... | collective-permute-start | bytes 1544 | tf_op jit(solution)/shard_map/while/body/eval_jaxpr/ppermute | solution.py:25
  187.3 7.4 collective-permute-start.7
  284.4 13.0 %collective-permute-start.4 = (f32[16,1,1024]{2,1,0:T(1,128)}, f32[16,1,1024]{2,1,0:T(1,128)S(1)}, u32[]{:S(2)}, u32[]{:S(2)}) collective-permute-start(f32[16,1,1024]{2,1,0:T(1,128)} %get-tuple-element.611), channel_id=1, source_target_pairs={{0,8},{8,16},{16,24},{1,9},{9,17},{17,25},{2,10},{10,18},{18,26},{... | collective-permute-start | bytes 196616 | tf_op jit(solution)/shard_map/while/body/eval_jaxpr/ppermute | solution.py:25
  285.7 11.7 %collective-permute-start.5 = (f32[16,1,1024]{2,1,0:T(1,128)}, f32[16,1,1024]{2,1,0:T(1,128)S(1)}, u32[]{:S(2)}, u32[]{:S(2)}) collective-permute-start(f32[16,1,1024]{2,1,0:T(1,128)} %get-tuple-element.612), channel_id=1, source_target_pairs={{8,0},{16,8},{24,16},{9,1},{17,9},{25,17},{10,2},{18,10},{26,18},{... | collective-permute-start | bytes 196616 | tf_op jit(solution)/shard_map/while/body/eval_jaxpr/ppermute | solution.py:26
  287.7 9.7 %collective-permute-start.6 = (f32[16,8,1]{2,1,0:T(8,128)}, f32[16,8,1]{2,1,0:T(8,128)S(1)}, u32[]{:S(2)}, u32[]{:S(2)}) collective-permute-start(f32[16,8,1]{2,1,0:T(8,128)} %get-tuple-element.613), channel_id=1, source_target_pairs={{0,1},{1,2},{2,3},{3,4},{4,5},{5,6},{6,7},{7,0},{8,9},{9,10},{10,1... | collective-permute-start | bytes 1544 | tf_op jit(solution)/shard_map/while/body/eval_jaxpr/ppermute | solution.py:25
  290.0 7.4 collective-permute-start.7
  386.7 11.2 %collective-permute-start.16 = (f32[16,8,1]{2,1,0:T(8,128)S(1)}, f32[16,8,1]{2,1,0:T(8,128)S(1)}, u32[]{:S(2)}, u32[]{:S(2)}) collective-permute-start(f32[16,8,1]{2,1,0:T(8,128)S(1)} %get-tuple-element.352), channel_id=1, source_target_pairs={{1,0},{2,1},{3,2},{4,3},{5,4},{6,5},{7,6},{0,7},{9,8},{10,9},{11,1... | collective-permute-start | bytes 1544 | tf_op jit(solution)/shard_map/ppermute | solution.py:26
  390.0 8.6 %collective-permute-start.18 = (f32[16,8,1]{2,1,0:T(8,128)S(1)}, f32[16,8,1]{2,1,0:T(8,128)S(1)}, u32[]{:S(2)}, u32[]{:S(2)}) collective-permute-start(f32[16,8,1]{2,1,0:T(8,128)S(1)} %get-tuple-element.353), channel_id=1, source_target_pairs={{0,1},{1,2},{2,3},{3,4},{4,5},{5,6},{6,7},{7,0},{8,9},{9,10},{10,1... | collective-permute-start | bytes 1544 | tf_op jit(solution)/shard_map/ppermute | solution.py:25
  390.0 7.9 %collective-permute-start.17 = (f32[16,1,1024]{2,1,0:T(1,128)S(1)}, f32[16,1,1024]{2,1,0:T(1,128)S(1)}, u32[]{:S(2)}, u32[]{:S(2)}) collective-permute-start(f32[16,1,1024]{2,1,0:T(1,128)S(1)} %get-tuple-element.354), channel_id=1, source_target_pairs={{8,0},{16,8},{24,16},{9,1},{17,9},{25,17},{10,2},{18,10},{26,18},{... | collective-permute-start | bytes 196616 | tf_op jit(solution)/shard_map/ppermute | solution.py:26
  391.3 3.5 copy-start.7
  391.3 3.5 copy-start.9
  391.3 3.5 copy-start.22
  391.4 7.3 collective-permute-start.19
  440.9 9.9 %copy-start.16 = (f32[16,16,128]{2,1,0:T(8,128)}, f32[16,16,128]{2,1,0:T(8,128)S(1)}, u32[]{:S(2)}) copy-start(f32[16,16,128]{2,1,0:T(8,128)S(1)} %get-tuple-element.723) | copy-start | bytes 393220 | tf_op jit(solution)/shard_map/while
  440.9 9.9 %copy-start.23 = (f32[16,128]{1,0:T(8,128)}, f32[16,128]{1,0:T(8,128)S(1)}, u32[]{:S(2)}) copy-start(f32[16,128]{1,0:T(8,128)S(1)} %get-tuple-element.730) | copy-start | bytes 24580 | tf_op jit(solution)/shard_map/while
  441.0 12.4 %collective-permute-start = (f32[16,1,1024]{2,1,0:T(1,128)S(1)}, f32[16,1,1024]{2,1,0:T(1,128)S(1)}, u32[]{:S(2)}, u32[]{:S(2)}) collective-permute-start(f32[16,1,1024]{2,1,0:T(1,128)S(1)} %get-tuple-element.584), channel_id=1, source_target_pairs={{0,8},{8,16},{16,24},{1,9},{9,17},{17,25},{2,10},{10,18},{18,26},{... | collective-permute-start | bytes 196616 | tf_op jit(solution)/shard_map/while/body/eval_jaxpr/ppermute | solution.py:25
  442.3 11.1 %collective-permute-start.1 = (f32[16,1,1024]{2,1,0:T(1,128)S(1)}, f32[16,1,1024]{2,1,0:T(1,128)S(1)}, u32[]{:S(2)}, u32[]{:S(2)}) collective-permute-start(f32[16,1,1024]{2,1,0:T(1,128)S(1)} %get-tuple-element.585), channel_id=1, source_target_pairs={{8,0},{16,8},{24,16},{9,1},{17,9},{25,17},{10,2},{18,10},{26,18},{... | collective-permute-start | bytes 196616 | tf_op jit(solution)/shard_map/while/body/eval_jaxpr/ppermute | solution.py:26
  443.7 9.7 %collective-permute-start.2 = (f32[16,8,1]{2,1,0:T(8,128)S(1)}, f32[16,8,1]{2,1,0:T(8,128)S(1)}, u32[]{:S(2)}, u32[]{:S(2)}) collective-permute-start(f32[16,8,1]{2,1,0:T(8,128)S(1)} %get-tuple-element.586), channel_id=1, source_target_pairs={{0,1},{1,2},{2,3},{3,4},{4,5},{5,6},{6,7},{7,0},{8,9},{9,10},{10,1... | collective-permute-start | bytes 1544 | tf_op jit(solution)/shard_map/while/body/eval_jaxpr/ppermute | solution.py:25
  446.0 7.4 collective-permute-start.3
  541.6 9.9 %copy-start.16 = (f32[16,16,128]{2,1,0:T(8,128)}, f32[16,16,128]{2,1,0:T(8,128)S(1)}, u32[]{:S(2)}) copy-start(f32[16,16,128]{2,1,0:T(8,128)S(1)} %get-tuple-element.723) | copy-start | bytes 393220 | tf_op jit(solution)/shard_map/while
  541.6 9.9 %copy-start.23 = (f32[16,128]{1,0:T(8,128)}, f32[16,128]{1,0:T(8,128)S(1)}, u32[]{:S(2)}) copy-start(f32[16,128]{1,0:T(8,128)S(1)} %get-tuple-element.730) | copy-start | bytes 24580 | tf_op jit(solution)/shard_map/while
  541.7 12.4 %collective-permute-start = (f32[16,1,1024]{2,1,0:T(1,128)S(1)}, f32[16,1,1024]{2,1,0:T(1,128)S(1)}, u32[]{:S(2)}, u32[]{:S(2)}) collective-permute-start(f32[16,1,1024]{2,1,0:T(1,128)S(1)} %get-tuple-element.584), channel_id=1, source_target_pairs={{0,8},{8,16},{16,24},{1,9},{9,17},{17,25},{2,10},{10,18},{18,26},{... | collective-permute-start | bytes 196616 | tf_op jit(solution)/shard_map/while/body/eval_jaxpr/ppermute | solution.py:25
  543.0 11.1 %collective-permute-start.1 = (f32[16,1,1024]{2,1,0:T(1,128)S(1)}, f32[16,1,1024]{2,1,0:T(1,128)S(1)}, u32[]{:S(2)}, u32[]{:S(2)}) collective-permute-start(f32[16,1,1024]{2,1,0:T(1,128)S(1)} %get-tuple-element.585), channel_id=1, source_target_pairs={{8,0},{16,8},{24,16},{9,1},{17,9},{25,17},{10,2},{18,10},{26,18},{... | collective-permute-start | bytes 196616 | tf_op jit(solution)/shard_map/while/body/eval_jaxpr/ppermute | solution.py:26
  544.4 9.7 %collective-permute-start.2 = (f32[16,8,1]{2,1,0:T(8,128)S(1)}, f32[16,8,1]{2,1,0:T(8,128)S(1)}, u32[]{:S(2)}, u32[]{:S(2)}) collective-permute-start(f32[16,8,1]{2,1,0:T(8,128)S(1)} %get-tuple-element.586), channel_id=1, source_target_pairs={{0,1},{1,2},{2,3},{3,4},{4,5},{5,6},{6,7},{7,0},{8,9},{9,10},{10,1... | collective-permute-start | bytes 1544 | tf_op jit(solution)/shard_map/while/body/eval_jaxpr/ppermute | solution.py:25
  546.7 7.4 collective-permute-start.3
  642.3 9.9 %copy-start.16 = (f32[16,16,128]{2,1,0:T(8,128)}, f32[16,16,128]{2,1,0:T(8,128)S(1)}, u32[]{:S(2)}) copy-start(f32[16,16,128]{2,1,0:T(8,128)S(1)} %get-tuple-element.723) | copy-start | bytes 393220 | tf_op jit(solution)/shard_map/while
  642.3 9.9 %copy-start.23 = (f32[16,128]{1,0:T(8,128)}, f32[16,128]{1,0:T(8,128)S(1)}, u32[]{:S(2)}) copy-start(f32[16,128]{1,0:T(8,128)S(1)} %get-tuple-element.730) | copy-start | bytes 24580 | tf_op jit(solution)/shard_map/while
  642.4 12.4 %collective-permute-start = (f32[16,1,1024]{2,1,0:T(1,128)S(1)}, f32[16,1,1024]{2,1,0:T(1,128)S(1)}, u32[]{:S(2)}, u32[]{:S(2)}) collective-permute-start(f32[16,1,1024]{2,1,0:T(1,128)S(1)} %get-tuple-element.584), channel_id=1, source_target_pairs={{0,8},{8,16},{16,24},{1,9},{9,17},{17,25},{2,10},{10,18},{18,26},{... | collective-permute-start | bytes 196616 | tf_op jit(solution)/shard_map/while/body/eval_jaxpr/ppermute | solution.py:25
  643.7 11.1 %collective-permute-start.1 = (f32[16,1,1024]{2,1,0:T(1,128)S(1)}, f32[16,1,1024]{2,1,0:T(1,128)S(1)}, u32[]{:S(2)}, u32[]{:S(2)}) collective-permute-start(f32[16,1,1024]{2,1,0:T(1,128)S(1)} %get-tuple-element.585), channel_id=1, source_target_pairs={{8,0},{16,8},{24,16},{9,1},{17,9},{25,17},{10,2},{18,10},{26,18},{... | collective-permute-start | bytes 196616 | tf_op jit(solution)/shard_map/while/body/eval_jaxpr/ppermute | solution.py:26
  645.0 9.7 %collective-permute-start.2 = (f32[16,8,1]{2,1,0:T(8,128)S(1)}, f32[16,8,1]{2,1,0:T(8,128)S(1)}, u32[]{:S(2)}, u32[]{:S(2)}) collective-permute-start(f32[16,8,1]{2,1,0:T(8,128)S(1)} %get-tuple-element.586), channel_id=1, source_target_pairs={{0,1},{1,2},{2,3},{3,4},{4,5},{5,6},{6,7},{7,0},{8,9},{9,10},{10,1... | collective-permute-start | bytes 1544 | tf_op jit(solution)/shard_map/while/body/eval_jaxpr/ppermute | solution.py:25
  647.3 7.4 collective-permute-start.3
  (33 other events, 39.8 us)
where the time goes:
time: 747 us; the launch traced here: 744 us
  blocking collectives  581 us (78%)
  starting transfers between devices  71.6 us (10%)
  matrix products  30.7 us (4%)
  other arithmetic  23.1 us (3%)
  local copies, waits for them, and re-layouts  18.3 us (2%)
  loops' own time  12.8 us (2%)
    psum x8, blocking collectives, squares(): return lax.psum(jnp.sum(vector * vector), ('lat', 'lon'))  330 us
    psum x6, blocking collectives, plain_step(): step_size = norm_prev / lax.psum(jnp.sum(direction * image), ('lat', 'lon'))  251 us
    ppermute x18, starting transfers between devices, with_halo(): after = lax.ppermute(leading, axis, down)  37.4 us
    ppermute x18, starting transfers between devices, with_halo(): before = lax.ppermute(last, axis, up)  30.8 us
  transfers between devices with their start and end apart: 37, of which 2 were waited for; matrix products, arithmetic and copies ran while one was open for 5% of the time, Pallas kernels for 0%

commit v1 on v0

v1 whole, which is shorter than its diff:
```python
import functools
import math

import jax
import jax.numpy as jnp
import numpy as np
from jax import lax
from jax.experimental import pallas as pl
from jax.experimental.pallas import tpu as pltpu
from jax.sharding import PartitionSpec as P

BLOCK = 128
CAP = 2
ITERS = 3
OUTER = 2
STEPS = ITERS * OUTER
MESH = pl.DeviceIdType.MESH
OMEGA_DEGREES = (28.984104, 30.0, 28.43973, 30.082137, 15.041069, 13.943036, 14.958931, 13.398661)
RATES = np.array(OMEGA_DEGREES, np.float32) * np.float32(math.pi / 180.0)
STIFF = np.float32(0.2) * (RATES / RATES[0]) ** 2


def sin_cos(angle):
    turn = jnp.floor(angle * (2.0 / math.pi) + 0.5)
    x = ((angle - turn * 1.5703125) - turn * 4.837512969970703125e-4) - turn * 7.54978995489188216e-8
    z = x * x
    s = ((-1.9515295891e-4 * z + 8.3321608736e-3) * z - 1.6666654611e-1) * z * x + x
    c = ((2.443315711809948e-5 * z - 1.388731625493765e-3) * z + 4.166664568298827e-2) * z * z - 0.5 * z + 1.0
    quarter = turn.astype(jnp.int32)
    odd = (quarter & 1) == 1
    sine = jnp.where(odd, c, s)
    cosine = jnp.where(odd, s, c)
    sine = jnp.where((quarter & 2) == 2, -sine, sine)
    cosine = jnp.where(((quarter + 1) & 2) == 2, -cosine, cosine)
    return sine, cosine


def kernel(
    nlat, nlon,
    route, tblk, depth, fric, mask, forc, ocell, otime, oval, oweight,
    x_out, r_out,
    dw, dwn, dws, dwe, dww, wetb, wetfric, coef, diag,
    payf, payi, outf, outi, inf, ini, plan, splan, mats, oslot,
    d, db, x, r, q, hd, hx, hr, hq, pk, sum_a, sum_b, send_b,
    hs, hrv, as_, ar, bs, br, os_, orv, ds_, dr, loc,
):
    rows, cols = depth.shape
    nblk = cols // BLOCK
    slots = nlon * CAP
    tiles = otime.shape[0]
    me_lat = lax.axis_index("lat")
    me_lon = lax.axis_index("lon")
    north, south = lax.rem(me_lat + 1, nlat), lax.rem(me_lat + nlat - 1, nlat)
    east, west = lax.rem(me_lon + 1, nlon), lax.rem(me_lon + nlon - 1, nlon)

    barrier = pltpu.get_barrier_semaphore()
    for k in range(1, nlon):
        pl.semaphore_signal(barrier, inc=1, device_id={"lon": lax.rem(me_lon + k, nlon)}, device_id_type=MESH)
    for k in range(1, nlat):
        pl.semaphore_signal(barrier, inc=1, device_id={"lat": lax.rem(me_lat + k, nlat)}, device_id_type=MESH)

    def remote(src, dst, send, recv, where):
        return pltpu.make_async_remote_copy(
            src_ref=src, dst_ref=dst, send_sem=send, recv_sem=recv, device_id=where, device_id_type=MESH
        )

    lane = lax.broadcasted_iota(jnp.int32, (1, BLOCK), 1)
    lane8 = lax.broadcasted_iota(jnp.int32, (8, BLOCK), 1)
    sub8 = lax.broadcasted_iota(jnp.int32, (8, BLOCK), 0)

    wet = mask[...].astype(jnp.float32)
    dw[...] = depth[...] * wet

    for t in range(tiles):
        payf[t, 0:1] = otime[t : t + 1]
        payf[t, 1:2] = oval[t : t + 1]
        payf[t, 2:3] = oweight[t : t + 1]
        payf[t, 3:4] = jnp.zeros((1, BLOCK), jnp.float32)
        payi[t] = jnp.broadcast_to(ocell[t : t + 1] + tblk[t] * BLOCK, (8, BLOCK))
    payf[tiles] = jnp.zeros((8, BLOCK), jnp.float32)
    payi[tiles] = jnp.zeros((8, BLOCK), jnp.int32)

    def pick(p, carry):
        first, second = jnp.int32(tiles), jnp.int32(tiles)
        for t in reversed(range(tiles)):
            hit = route[t, 0] == p
            second = jnp.where(hit, first, second)
            first = jnp.where(hit, jnp.int32(t), first)
        one, two = payf[first], payf[second]
        outf[p] = jnp.concatenate([one[0:4], two[0:4]], axis=0)
        outi[p] = jnp.where(sub8 == 0, payi[first], payi[second])
        return carry

    lax.fori_loop(0, nlon, pick, 0)
    pl.semaphore_wait(barrier, nlon + nlat - 2)

    first_copies = [
        remote(dw, dws, ds_.at[0], dr.at[0], {"lat": north}),
        remote(dw, dwn, ds_.at[1], dr.at[1], {"lat": south}),
        remote(dw.at[:, pl.ds(0, BLOCK)], dwe, ds_.at[2], dr.at[2], {"lon": west}),
        remote(dw.at[:, pl.ds(cols - BLOCK, BLOCK)], dww, ds_.at[3], dr.at[3], {"lon": east}),
    ]

    def obs_copy(k):
        peer = lax.rem(me_lon + k, nlon)
        return [
            remote(outf.at[peer], inf.at[me_lon], os_.at[0, peer], orv.at[0, me_lon], {"lon": peer}),
            remote(outi.at[peer], ini.at[me_lon], os_.at[1, peer], orv.at[1, me_lon], {"lon": peer}),
        ]

    def obs_wait(k):
        peer = lax.rem(me_lon + k, nlon)
        remote(outf.at[peer], inf.at[peer], os_.at[0, peer], orv.at[0, peer], {"lon": peer}).wait_recv()
        remote(outi.at[peer], ini.at[peer], os_.at[1, peer], orv.at[1, peer], {"lon": peer}).wait_recv()

    obs_sends = [c for k in range(1, nlon) for c in obs_copy(k)]
    for c in obs_sends:
        c.start()
    for c in first_copies:
        c.start()
    inf[me_lon] = outf[me_lon]
    ini[me_lon] = outi[me_lon]

    for cb in range(nblk):
        at = pl.ds(cb * BLOCK, BLOCK)
        for h in range(2):
            r[pl.ds(1, rows), h, :, at] = jnp.swapaxes(forc[h, :, :, at], 0, 1)
    x[...] = jnp.zeros_like(x)
    hx[...] = jnp.zeros_like(hx)
    oslot[slots] = jnp.zeros((2, 8, BLOCK), jnp.float32)

    for c in first_copies:
        c.wait_recv()
    a = dw[...]
    colid = lax.broadcasted_iota(jnp.int32, (rows, cols), 1)
    rowid = lax.broadcasted_iota(jnp.int32, (rows, cols), 0)
    keep_n = (me_lat < nlat - 1).astype(jnp.float32)
    keep_s = (me_lat > 0).astype(jnp.float32)

    def harmonic(first, second):
        return 2.0 * first * second / jnp.maximum(first + second, 0.5)

    side = harmonic(a, jnp.where(colid == cols - 1, dwe[:, 0:1], pltpu.roll(a, cols - 1, 1)))
    total = side
    for row in range(rows):
        coef[0, row] = jnp.broadcast_to(side[row : row + 1], (8, cols))
    side = harmonic(a, jnp.where(colid == 0, dww[:, BLOCK - 1 : BLOCK], pltpu.roll(a, 1, 1)))
    total = total + side
    for row in range(rows):
        coef[1, row] = jnp.broadcast_to(side[row : row + 1], (8, cols))
    side = harmonic(a, jnp.where(rowid == rows - 1, dwn[0:1, :] * keep_n, pltpu.roll(a, rows - 1, 0)))
    total = total + side
    for row in range(rows):
        coef[2, row] = jnp.broadcast_to(side[row : row + 1], (8, cols))
    side = harmonic(a, jnp.where(rowid == 0, dws[rows - 1 : rows, :] * keep_s, pltpu.roll(a, 1, 0)))
    total = total + side
    for row in range(rows):
        coef[3, row] = jnp.broadcast_to(side[row : row + 1], (8, cols))
    stiff = jnp.zeros((8, 1), jnp.float32)
    rate = jnp.zeros((8, BLOCK), jnp.float32)
    sub1 = lax.broadcasted_iota(jnp.int32, (8, 1), 0)
    for c in range(8):
        stiff = jnp.where(sub1 == c, float(STIFF[c]), stiff)
        rate = jnp.where(sub8 == c, float(RATES[c]), rate)
    drag = fric[...]
    total = total + wet * drag + (1.0 - wet)
    for row in range(rows):
        wide = jnp.broadcast_to(wet[row : row + 1], (8, cols))
        wetb[row] = wide
        wetfric[row] = wide * jnp.broadcast_to(drag[row : row + 1], (8, cols))
        diag[row] = wide * stiff + jnp.broadcast_to(total[row : row + 1], (8, cols))

    for k in range(1, nlon):
        obs_wait(k)
    rep = jnp.full((1, BLOCK), slots, jnp.int32)
    homes = jnp.full((1, BLOCK), -1, jnp.int32)
    for s in reversed(range(slots)):
        home = ini[s // CAP, pl.ds(s % CAP, 1), :] >> 7
        rep = jnp.where(home == lane, s, rep)
        homes = jnp.where(lane == s, home, homes)
    chain = jnp.full((1, BLOCK), slots, jnp.int32)
    for s in reversed(range(slots)):
        home = ini[s // CAP, pl.ds(s % CAP, 1), :] >> 7
        chain = jnp.where((home == homes) & (lane < s), s, chain)
    plan[...] = jnp.where(
        sub8 == 0,
        jnp.broadcast_to(homes, (8, BLOCK)),
        jnp.where(sub8 == 1, jnp.broadcast_to(chain, (8, BLOCK)), jnp.broadcast_to(rep, (8, BLOCK))),
    )
    to_scalars = pltpu.make_async_copy(plan, splan, loc.at[0])
    to_scalars.start()

    cells = lax.broadcasted_iota(jnp.int32, (BLOCK, BLOCK), 0)

    def build(o, carry):
        for k in range(CAP):
            times = inf[o, pl.ds(4 * k, 1), :]
            value = inf[o, pl.ds(4 * k + 1, 1), :]
            weight = inf[o, pl.ds(4 * k + 2, 1), :]
            cell = ini[o, pl.ds(k, 1), :] & (BLOCK - 1)
            sine, cosine = sin_cos(rate * times)
            basis = (cosine, sine)
            weighted = (weight * cosine, weight * sine)
            parts = []
            for h in range(2):
                for c in range(8):
                    one = weighted[h][c : c + 1]
                    parts.append(one * basis[0])
                    parts.append(one * basis[1])
            parts.append(weighted[0] * value)
            parts.append(weighted[1] * value)
            terms = jnp.concatenate(parts, axis=0)
            high = terms.astype(jnp.bfloat16)
            low = (terms - high.astype(jnp.float32)).astype(jnp.bfloat16)
            hot = (cells == cell).astype(jnp.float32).astype(jnp.bfloat16)
            mats[o * CAP + k] = lax.dot_general(
                jnp.concatenate([high, low], axis=1),
                jnp.concatenate([hot, hot], axis=1),
                (((1,), (1,)), ((), ())),
                preferred_element_type=jnp.float32,
            )
        return carry

    lax.fori_loop(0, nlon, build, 0)
    to_scalars.wait()

    def first_slots(i, carry):
        s = slots - 1 - i
        after = oslot[splan[1, s]]
        oslot[s] = mats[s, 256:272, :].reshape(2, 8, BLOCK) + after
        return carry

    lax.fori_loop(0, slots, first_slots, 0)

    def pack(row, col, value, packed):
        shift = row if col == 0 else row + 1
        moved = pltpu.roll(value, shift, 2)
        return jnp.where(lane8 == row, moved, packed)

    zero = jnp.zeros((2, 8, BLOCK), jnp.float32)

    def start_rhs(row, carry):
        lo, hi = carry
        for cb in range(nblk):
            at = pl.ds(cb * BLOCK, BLOCK)
            v = wetb[row, :, at] * r[row + 1, :, :, at] + oslot[splan[2, row * nblk + cb]]
            r[row + 1, :, :, at] = v
            q[STEPS, row + 1, :, :, at] = v
            db[(row + 1) * nblk + cb] = v
            if cb == 0:
                lo = pack(row, 0, v, lo)
            if cb == nblk - 1:
                hi = pack(row, 1, v, hi)
        return lo, hi

    lo, hi = lax.fori_loop(0, rows, start_rhs, (zero, zero))
    pk[STEPS, 0] = lo
    pk[STEPS, 1] = hi

    def halo(i):
        return [
            remote(q.at[i, 1], q.at[i, rows + 1], hs.at[i, 0], hrv.at[i, 0], {"lat": south}),
            remote(q.at[i, rows], q.at[i, 0], hs.at[i, 1], hrv.at[i, 1], {"lat": north}),
            remote(pk.at[i, 0], hq.at[i, 1], hs.at[i, 2], hrv.at[i, 2], {"lon": west}),
            remote(pk.at[i, 1], hq.at[i, 0], hs.at[i, 3], hrv.at[i, 3], {"lon": east}),
        ]

    def begin(i):
        for c in halo(i):
            c.start()
        d[pl.ds(1, rows)] = r[pl.ds(1, rows)]
        for c in halo(i):
            c.wait()
        for edge in (0, rows + 1):
            d[edge] = q[i, edge]
            r[edge] = q[i, edge]
        hd[...] = hq[i]
        hr[...] = hq[i]

    def all_sum(i, part):
        sum_a[i, me_lat] = part
        for k in range(1, nlat):
            peer = lax.rem(me_lat + k, nlat)
            remote(sum_a.at[i, me_lat], sum_a.at[i, me_lat], as_.at[i, peer], ar.at[i, me_lat], {"lat": peer}).start()
        for k in range(1, nlat):
            peer = lax.rem(me_lat + k, nlat)
            remote(sum_a.at[i, peer], sum_a.at[i, peer], as_.at[i, peer], ar.at[i, peer], {"lat": peer}).wait_recv()
        part = sum_a[i, 0]
        for k in range(1, nlat):
            part = part + sum_a[i, k]
        sum_b[i, me_lon] = part
        for k in range(1, nlon):
            peer = lax.rem(me_lon + k, nlon)
            remote(sum_b.at[i, me_lon], sum_b.at[i, me_lon], bs.at[i, peer], br.at[i, me_lon], {"lon": peer}).start()
        for k in range(1, nlon):
            peer = lax.rem(me_lon + k, nlon)
            remote(sum_b.at[i, peer], sum_b.at[i, peer], bs.at[i, peer], br.at[i, peer], {"lon": peer}).wait_recv()
        part = sum_b[i, 0]
        for k in range(1, nlon):
            part = part + sum_b[i, k]
        return jnp.sum(part, axis=1, keepdims=True)

    def sides(ref, halos, row):
        v = [ref[row + 1, :, :, pl.ds(cb * BLOCK, BLOCK)] for cb in range(nblk)]
        to_west = [pltpu.roll(b, BLOCK - 1, 2) for b in v]
        to_west.append(pltpu.roll(halos[1], BLOCK - 1 - row, 2))
        to_east = [pltpu.roll(halos[0], BLOCK - row, 2)] + [pltpu.roll(b, 1, 2) for b in v]
        e = [jnp.where(lane8 == BLOCK - 1, to_west[cb + 1], to_west[cb]) for cb in range(nblk)]
        w = [jnp.where(lane8 == 0, to_east[cb], to_east[cb + 1]) for cb in range(nblk)]
        return v, e, w

    def step(i, carry):
        def slot(j, carry):
            s = slots - 1 - j
            after = oslot[splan[1, s]]
            v = db[splan[0, s] + nblk]
            acc = [after, zero]
            for c in range(16):
                m = mats[s, 16 * c : 16 * c + 16, :].reshape(2, 8, BLOCK)
                acc[c % 2] = acc[c % 2] + m * v[c // 8, c % 8 : c % 8 + 1, :]
            oslot[s] = acc[0] + acc[1]
            return carry

        lax.fori_loop(0, slots, slot, 0)

        def line(row, carry):
            lo, hi, rr, rq, dq, qq = carry
            v, e, w = sides(d, hd, row)
            for cb in range(nblk):
                at = pl.ds(cb * BLOCK, BLOCK)
                image = (
                    diag[row, :, at] * v[cb]
                    - coef[0, row, :, at] * e[cb]
                    - coef[1, row, :, at] * w[cb]
                    - coef[2, row, :, at] * d[row + 2, :, :, at]
                    - coef[3, row, :, at] * d[row, :, :, at]
                    + oslot[splan[2, row * nblk + cb]]
                )
                q[i, row + 1, :, :, at] = image
                res = r[row + 1, :, :, at]
                rr = rr + res * res
                rq = rq + res * image
                dq = dq + v[cb] * image
                qq = qq + image * image
                if cb == 0:
                    lo = pack(row, 0, image, lo)
                if cb == nblk - 1:
                    hi = pack(row, 1, image, hi)
            return lo, hi, rr, rq, dq, qq

        lo, hi, *sums = lax.fori_loop(0, rows, line, (zero,) * 6)
        pk[i, 0] = lo
        pk[i, 1] = hi
        part = jnp.zeros((8, BLOCK), jnp.float32)
        for k, s in enumerate(sums):
            part = jnp.where(sub8 == k, jnp.sum(s[0] + s[1], axis=0, keepdims=True), part)
        for c in halo(i):
            c.start()
        whole = all_sum(i, part)
        rr, rq, dq, qq = (whole[k : k + 1] for k in range(4))
        size = rr / dq
        beta = (rr - 2.0 * size * rq + size * size * qq) / rr
        for c in halo(i):
            c.wait()

        def update(row, carry):
            for cb in range(nblk):
                at = pl.ds(cb * BLOCK, BLOCK)
                old = d[row, :, :, at]
                x[row, :, :, at] = x[row, :, :, at] + size * old
                res = r[row, :, :, at] - size * q[i, row, :, :, at]
                r[row, :, :, at] = res
                new = res + beta * old
                d[row, :, :, at] = new
                db[row * nblk + cb] = new
            return carry

        lax.fori_loop(0, rows + 2, update, 0)
        hx[...] = hx[...] + size * hd[...]
        hr[...] = hr[...] - size * hq[i]
        hd[...] = hr[...] + beta * hd[...]
        for k in range(1, nlat):
            peer = lax.rem(me_lat + k, nlat)
            remote(sum_a.at[i, me_lat], sum_a.at[i, me_lat], as_.at[i, peer], ar.at[i, me_lat], {"lat": peer}).wait_send()
        for k in range(1, nlon):
            peer = lax.rem(me_lon + k, nlon)
            remote(sum_b.at[i, me_lon], sum_b.at[i, me_lon], bs.at[i, peer], br.at[i, me_lon], {"lon": peer}).wait_send()
        return carry

    begin(STEPS)
    for c in obs_sends + first_copies:
        c.wait_send()
    lax.fori_loop(0, ITERS, step, 0)

    def friction(row, carry):
        lo, hi = carry
        v, e, _ = sides(x, hx, row)
        for cb in range(nblk):
            at = pl.ds(cb * BLOCK, BLOCK)
            flux_e = coef[0, row, :, at] * (e[cb] - v[cb])
            flux_n = coef[2, row, :, at] * (x[row + 2, :, :, at] - v[cb])
            square = flux_e * flux_e + flux_n * flux_n
            speed = jnp.sum(square[0] + square[1], axis=0, keepdims=True)
            extra = wetfric[row, :, at] * (jnp.sqrt(1.0 + speed / 16.0) - 1.0)
            diag[row, :, at] = diag[row, :, at] + extra
            res = r[row + 1, :, :, at] - extra * v[cb]
            r[row + 1, :, :, at] = res
            q[STEPS + 1, row + 1, :, :, at] = res
            db[(row + 1) * nblk + cb] = res
            if cb == 0:
                lo = pack(row, 0, res, lo)
            if cb == nblk - 1:
                hi = pack(row, 1, res, hi)
        return lo, hi

    lo, hi = lax.fori_loop(0, rows, friction, (zero, zero))
    pk[STEPS + 1, 0] = lo
    pk[STEPS + 1, 1] = hi
    begin(STEPS + 1)
    lax.fori_loop(ITERS, STEPS, step, 0)

    for cb in range(nblk):
        at = pl.ds(cb * BLOCK, BLOCK)
        for h in range(2):
            x_out[h, :, :, at] = jnp.swapaxes(x[pl.ds(1, rows), h, :, at], 0, 1)
            r_out[h, :, :, at] = jnp.swapaxes(r[pl.ds(1, rows), h, :, at], 0, 1)


def shards(nlat, nlon, depth, friction, ocean_mask, forcing, tile_route, tile_block, obs_cell, obs_time, obs_value, obs_weight):
    channels, rows, cols = forcing.shape
    slots = nlon * CAP
    nblk, tiles = cols // BLOCK, obs_time.shape[0]
    f32, i32 = jnp.float32, jnp.int32
    vmem = pl.BlockSpec(memory_space=pltpu.VMEM)
    smem = pl.BlockSpec(memory_space=pltpu.SMEM)
    field = (rows + 2, 2, 8, cols)
    dma = pltpu.SemaphoreType.DMA
    scratch = [
        pltpu.VMEM((rows, cols), f32),
        pltpu.VMEM((rows, cols), f32),
        pltpu.VMEM((rows, cols), f32),
        pltpu.VMEM((rows, BLOCK), f32),
        pltpu.VMEM((rows, BLOCK), f32),
        pltpu.VMEM((rows, 8, cols), f32),
        pltpu.VMEM((rows, 8, cols), f32),
        pltpu.VMEM((4, rows, 8, cols), f32),
        pltpu.VMEM((rows, 8, cols), f32),
        pltpu.VMEM((tiles + 1, 8, BLOCK), f32),
        pltpu.VMEM((tiles + 1, 8, BLOCK), i32),
        pltpu.VMEM((nlon, 8, BLOCK), f32),
        pltpu.VMEM((nlon, 8, BLOCK), i32),
        pltpu.VMEM((nlon, 8, BLOCK), f32),
        pltpu.VMEM((nlon, 8, BLOCK), i32),
        pltpu.VMEM((8, BLOCK), i32),
        pltpu.SMEM((8, BLOCK), i32),
        pltpu.VMEM((slots, 272, BLOCK), f32),
        pltpu.VMEM((slots + 1, 2, 8, BLOCK), f32),
        pltpu.VMEM(field, f32),
        pltpu.VMEM(((rows + 2) * nblk, 2, 8, BLOCK), f32),
        pltpu.VMEM(field, f32),
        pltpu.VMEM(field, f32),
        pltpu.VMEM((STEPS + 2,) + field, f32),
        pltpu.VMEM((2, 2, 8, BLOCK), f32),
        pltpu.VMEM((2, 2, 8, BLOCK), f32),
        pltpu.VMEM((2, 2, 8, BLOCK), f32),
        pltpu.VMEM((STEPS + 2, 2, 2, 8, BLOCK), f32),
        pltpu.VMEM((STEPS + 2, 2, 2, 8, BLOCK), f32),
        pltpu.VMEM((STEPS, nlat, 8, BLOCK), f32),
        pltpu.VMEM((STEPS, nlon, 8, BLOCK), f32),
        pltpu.VMEM((8, BLOCK), f32),
        dma((STEPS + 2, 4)),
        dma((STEPS + 2, 4)),
        dma((STEPS, nlat)),
        dma((STEPS, nlat)),
        dma((STEPS, nlon)),
        dma((STEPS, nlon)),
        dma((2, nlon)),
        dma((2, nlon)),
        dma((4,)),
        dma((4,)),
        dma((1,)),
    ]
    shape = jax.ShapeDtypeStruct((2, channels // 2, rows, cols), f32)
    x, r = pl.pallas_call(
        functools.partial(kernel, nlat, nlon),
        out_shape=(shape, shape),
        in_specs=[smem, smem] + [vmem] * 8,
        out_specs=(vmem, vmem),
        scratch_shapes=scratch,
        compiler_params=pltpu.CompilerParams(
            collective_id=0, has_side_effects=True, vmem_limit_bytes=40 * 2**20
        ),
    )(
        tile_route, tile_block, depth, friction, ocean_mask, forcing.reshape(2, channels // 2, rows, cols),
        obs_cell, obs_time, obs_value, obs_weight,
    )
    return x.reshape(forcing.shape), r.reshape(forcing.shape)


def solution(mesh):
    tile = P(("lat", "lon"), None)
    grid = P("lat", "lon")
    in_specs = (grid, grid, grid, P(None, "lat", "lon"), tile, P(("lat", "lon")), tile, tile, tile, tile)
    out_specs = (P(None, "lat", "lon"), P(None, "lat", "lon"))
    body = functools.partial(shards, mesh.shape["lat"], mesh.shape["lon"])
    return jax.shard_map(body, mesh=mesh, in_specs=in_specs, out_specs=out_specs, check_vma=False)
```

time: 747 us -> 92.6 us (0.12)
  blocking collectives: 581 us -> 0 us
  Pallas kernels: 0 us -> 83.7 us
  starting transfers between devices: 71.6 us -> 0 us
  matrix products: 30.7 us -> 0 us
  other arithmetic: 23.1 us -> 0 us
  loops' own time: 12.8 us -> 0 us
  local copies, waits for them, and re-layouts: 18.3 us -> 7.74 us
    psum x14 -> x0, blocking collectives: 581 us -> none  [the longest x8 330 us: squares(): return lax.psum(jnp.sum(vector * vector), ('lat', 'lon'))]
    pallas_call x0 -> x1, Pallas kernels: none -> 83.7 us  [shards(): pl.pallas_call(functools.partial(kernel, nlat, nlon), out_shape=(shape, s...]
    ppermute x36 -> x0, starting transfers between devices: 68.3 us -> none  [the longest x18 37.4 us: with_halo(): after = lax.ppermute(leading, axis, down)]
    dot_general x35 -> x0, matrix products: 30.7 us -> none  [the longest x8 13.1 us: observe(): jnp.einsum('sck,sok->sco', block_field, cell_hot, precision=HIGHEST)]
    reduce_sum x17 -> x0, other arithmetic: 18.9 us -> none  [the longest x6 9.7 us: plain_step(): step_size = norm_prev / lax.psum(jnp.sum(direction * image), ('lat', 'lon'))]
    another operation x2 -> x0, loops' own time: 12.8 us -> none  [shards(): lax.fori_loop(0, ITERS, plain_step, (elevation, residual, residual, norm_...]
  transfers between devices with their start and end apart: 37 -> 0, of which waited for: 2 -> 0; matrix products, arithmetic and copies ran while one was open for 5% -> 0% of each run, Pallas kernels for 0% -> 0%
where the time goes in v1:
time: 92.6 us; the launch traced here: 92.1 us
  Pallas kernels  83.7 us (90%)
  local copies, waits for them, and re-layouts  7.74 us (8%)
    pallas_call x1, Pallas kernels, shards(): pl.pallas_call(functools.partial(kernel, nlat, nlon), out_shape=(shape, s...  83.7 us
    unnamed x21, local copies, waits for them, and re-layouts  7.74 us

profile of v1, /device:TPU:0, one launch (start us, length us, event | category | flops | bytes accessed | tf_op | source)
XLA Modules:
  0.0 92.1 jit_solution(18339710699338191814)
XLA Ops:
  0.6 0.0 copy-start.4
  0.6 0.0 copy-start.8
  0.7 0.7 copy.12.route
  1.4 0.0 copy-done.4
  1.4 0.0 copy-done.8
  1.4 0.0 copy-start
  1.4 1.0 %copy-done = f32[16,8,1024]{2,1,0:T(8,128)S(1)} copy-done((f32[16,8,1024]{2,1,0:T(8,128)S(1)}, f32[16,8,1024]{2,1,0:T(8,128)}, u32[]{:S(2)}) %copy-start) | copy-done | bytes 524312
  2.4 0.0 copy-start.1
  2.4 0.8 copy-done.1
  3.2 0.0 copy-start.2
  3.2 0.8 copy-done.2
  4.0 0.0 copy-start.3
  4.0 0.8 copy-done.3
  4.7 0.0 copy-start.5
  4.7 0.7 copy-done.5
  5.4 0.0 copy-start.6
  5.4 0.7 copy-done.6
  6.1 0.0 copy-start.7
  6.1 0.7 copy-done.7
  6.8 83.7 %shard_map.113 = (f32[2,8,8,1024]{3,2,1,0:T(8,128)S(1)}, f32[2,8,8,1024]{3,2,1,0:T(8,128)S(1)}) custom-call(s32[16,1]{1,0:T(8,128)S(1)} %copy.12.route, s32[16]{0:T(128)S(1)} %copy-done.8, f32[8,1024]{1,0:T(8,128)S(1)} %copy-done.1, f32[8,1024]{1,0:T(8,128)S(1)} %copy-done.2, s32[8,1024]{1,0:T(8,128)S(1)} %copy-done.3, f32[2,8,8,1024]{3,2,1,0:T(8,128)S(1)} %bitcast.3, ...), custom_call_target="tpu_custom_call" | custom-call | tf_op jit(solution)/shard_map/pallas_call | solution.py:484
  90.5 0.8 copy.15
  91.3 0.8 copy.16
Async XLA Ops:
  0.6 0.8 copy-start.4
  0.6 0.8 copy-start.8
  1.4 1.0 %copy-start = (f32[16,8,1024]{2,1,0:T(8,128)S(1)}, f32[16,8,1024]{2,1,0:T(8,128)}, u32[]{:S(2)}) copy-start(f32[16,8,1024]{2,1,0:T(8,128)} %param.13) | copy-start | bytes 1572868
  2.4 0.8 copy-start.1
  3.2 0.8 copy-start.2
  4.0 0.8 copy-start.3
  4.7 0.7 copy-start.5
  5.4 0.7 copy-start.6
  6.1 0.7 copy-start.7

commit v2 on v1

--- a/solution.py
+++ b/solution.py
@@ -37,6 +37,15 @@
 
 def kernel(
     nlat, nlon,
+    route, tblk, *refs,
+):
+    sources, refs = refs[:8], refs[8:]
+    landed = refs[-9:-1]
+    work(nlat, nlon, sources, refs[-1], route, tblk, *landed, *refs[:-9])
+
+
+def work(
+    nlat, nlon, sources, load,
     route, tblk, depth, fric, mask, forc, ocell, otime, oval, oweight,
     x_out, r_out,
     dw, dwn, dws, dwe, dww, wetb, wetfric, coef, diag,
@@ -53,6 +62,12 @@
     north, south = lax.rem(me_lat + 1, nlat), lax.rem(me_lat + nlat - 1, nlat)
     east, west = lax.rem(me_lon + 1, nlon), lax.rem(me_lon + nlon - 1, nlon)
 
+    loads = [
+        pltpu.make_async_copy(src, dst, load.at[k])
+        for k, (src, dst) in enumerate(zip(sources, (depth, fric, mask, forc, ocell, otime, oval, oweight)))
+    ]
+    for c in loads:
+        c.start()
     barrier = pltpu.get_barrier_semaphore()
     for k in range(1, nlon):
         pl.semaphore_signal(barrier, inc=1, device_id={"lon": lax.rem(me_lon + k, nlon)}, device_id_type=MESH)
@@ -68,6 +83,8 @@
     lane8 = lax.broadcasted_iota(jnp.int32, (8, BLOCK), 1)
     sub8 = lax.broadcasted_iota(jnp.int32, (8, BLOCK), 0)
 
+    for c in loads:
+        c.wait()
     wet = mask[...].astype(jnp.float32)
     dw[...] = depth[...] * wet
 
@@ -354,14 +371,22 @@
         part = jnp.zeros((8, BLOCK), jnp.float32)
         for k, s in enumerate(sums):
             part = jnp.where(sub8 == k, jnp.sum(s[0] + s[1], axis=0, keepdims=True), part)
-        for c in halo(i):
-            c.start()
+        more = lax.rem(i, ITERS) < ITERS - 1
+
+        @pl.when(more)
+        def _():
+            for c in halo(i):
+                c.start()
+
         whole = all_sum(i, part)
         rr, rq, dq, qq = (whole[k : k + 1] for k in range(4))
         size = rr / dq
         beta = (rr - 2.0 * size * rq + size * size * qq) / rr
-        for c in halo(i):
-            c.wait()
+
+        @pl.when(more)
+        def _():
+            for c in halo(i):
+                c.wait()
 
         def update(row, carry):
             for cb in range(nblk):
@@ -479,12 +504,21 @@
         dma((4,)),
         dma((4,)),
         dma((1,)),
+        pltpu.VMEM((rows, cols), f32),
+        pltpu.VMEM((rows, cols), f32),
+        pltpu.VMEM((rows, cols), i32),
+        pltpu.VMEM((2, channels // 2, rows, cols), f32),
+        pltpu.VMEM((tiles, BLOCK), i32),
+        pltpu.VMEM((tiles, BLOCK), f32),
+        pltpu.VMEM((tiles, BLOCK), f32),
+        pltpu.VMEM((tiles, BLOCK), f32),
+        dma((8,)),
     ]
     shape = jax.ShapeDtypeStruct((2, channels // 2, rows, cols), f32)
     x, r = pl.pallas_call(
         functools.partial(kernel, nlat, nlon),
         out_shape=(shape, shape),
-        in_specs=[smem, smem] + [vmem] * 8,
+        in_specs=[smem, smem] + [pl.BlockSpec(memory_space=pltpu.HBM)] * 8,
         out_specs=(vmem, vmem),
         scratch_shapes=scratch,
         compiler_params=pltpu.CompilerParams(

time: 92.6 us -> 91.5 us (0.988)
  Pallas kernels: 83.7 us -> 82.5 us
    pallas_call x1, Pallas kernels: 83.7 us -> 82.5 us  [shards(): pl.pallas_call(functools.partial(kernel, nlat, nlon), out_shape=(shape, s...]
where the time goes in v2:
time: 91.5 us; the launch traced here: 91 us
  Pallas kernels  82.5 us (90%)
  local copies, waits for them, and re-layouts  7.74 us (8%)
    pallas_call x1, Pallas kernels, shards(): pl.pallas_call(functools.partial(kernel, nlat, nlon), out_shape=(shape, s...  82.5 us
    unnamed x21, local copies, waits for them, and re-layouts  7.74 us

profile of v2, /device:TPU:0, one launch (start us, length us, event | category | flops | bytes accessed | tf_op | source)
XLA Modules:
  0.0 91.0 jit_solution(12932322863178324801)
XLA Ops:
  0.6 0.0 copy-start.4
  0.6 0.0 copy-start.8
  0.7 0.7 copy.12.route
  1.4 0.0 copy-done.4
  1.4 0.0 copy-done.8
  1.4 0.0 copy-start
  1.4 1.0 %copy-done = f32[16,8,1024]{2,1,0:T(8,128)S(1)} copy-done((f32[16,8,1024]{2,1,0:T(8,128)S(1)}, f32[16,8,1024]{2,1,0:T(8,128)}, u32[]{:S(2)}) %copy-start) | copy-done | bytes 524312
  2.4 0.0 copy-start.1
  2.4 0.8 copy-done.1
  3.2 0.0 copy-start.2
  3.2 0.8 copy-done.2
  4.0 0.0 copy-start.3
  4.0 0.8 copy-done.3
  4.7 0.0 copy-start.5
  4.7 0.7 copy-done.5
  5.4 0.0 copy-start.6
  5.4 0.7 copy-done.6
  6.1 0.0 copy-start.7
  6.1 0.7 copy-done.7
  6.8 82.5 %shard_map.113 = (f32[2,8,8,1024]{3,2,1,0:T(8,128)S(1)}, f32[2,8,8,1024]{3,2,1,0:T(8,128)S(1)}) custom-call(s32[16,1]{1,0:T(8,128)S(1)} %copy.12.route, s32[16]{0:T(128)S(1)} %copy-done.8, f32[8,1024]{1,0:T(8,128)S(1)} %copy-done.1, f32[8,1024]{1,0:T(8,128)S(1)} %copy-done.2, s32[8,1024]{1,0:T(8,128)S(1)} %copy-done.3, f32[2,8,8,1024]{3,2,1,0:T(8,128)S(1)} %bitcast.3, ...), custom_call_target="tpu_custom_call" | custom-call | tf_op jit(solution)/shard_map/pallas_call | solution.py:518
  89.4 0.8 copy.15
  90.2 0.8 copy.16
Async XLA Ops:
  0.6 0.8 copy-start.4
  0.6 0.8 copy-start.8
  1.4 1.0 %copy-start = (f32[16,8,1024]{2,1,0:T(8,128)S(1)}, f32[16,8,1024]{2,1,0:T(8,128)}, u32[]{:S(2)}) copy-start(f32[16,8,1024]{2,1,0:T(8,128)} %param.13) | copy-start | bytes 1572868
  2.4 0.8 copy-start.1
  3.2 0.8 copy-start.2
  4.0 0.8 copy-start.3
  4.7 0.7 copy-start.5
  5.4 0.7 copy-start.6
  6.1 0.7 copy-start.7
